TPU v7x, 32 devices: a whole 2x2x4 slice. The times are simulated.
32 devices in a mesh: dp: 4 (over z), fsdp: 8 (over y, x, core).
Axes of the slice: x: 2, y: 2, z: 4, core: 2. Of those that a mesh axis runs over, the one named last changes fastest.
Arguments:
- tokens: bfloat16 [64, 512, 768], P('dp', 'fsdp'), may hold values from -6 to 6
- cotangent: bfloat16 [64, 512, 768], P('dp', 'fsdp'), may hold values from -6 to 6
- key_mask: int32 [64, 512], P('dp', 'fsdp'), may hold values from 0 to 1, as said below
- seq_lengths: int32 [64], P(('dp', 'fsdp')), may hold values from 257 to 512, as said below
- block_pattern: int32 [12], replicated, may hold values from 0 to 1, as said below
- deal_order: int32 [4, 16], P('dp'), may hold values from 0 to 15, each once within a row
- qkv_weight: bfloat16 [768, 2304], P(('dp', 'fsdp')), may hold values from -0.21875 to 0.21875
- out_weight: bfloat16 [768, 768], P(('dp', 'fsdp')), may hold values from -2.5 to 2.5
- up_weight: bfloat16 [768, 3072], P(('dp', 'fsdp')), may hold values from -0.21875 to 0.21875
- down_weight: bfloat16 [3072, 768], P(('dp', 'fsdp')), may hold values from -0.109375 to 0.109375
- query_bias: bfloat16 [768], P(('dp', 'fsdp')), may hold values from -3 to 3
- value_bias: bfloat16 [768], P(('dp', 'fsdp')), may hold values from -0.29882812 to 0.29882812
- out_bias: bfloat16 [768], P(('dp', 'fsdp')), may hold values from -2 to 2
- up_bias: bfloat16 [3072], P(('dp', 'fsdp')), may hold values from -2 to 2
- down_bias: bfloat16 [768], P(('dp', 'fsdp')), may hold values from -2 to 2
- attn_gain: bfloat16 [768], P(('dp', 'fsdp')), may hold values from 0.5 to 1.5
- attn_shift: bfloat16 [768], P(('dp', 'fsdp')), may hold values from -1.1953125 to 1.1953125
- ffn_gain: bfloat16 [768], P(('dp', 'fsdp')), may hold values from 0.5 to 1.5
- ffn_shift: bfloat16 [768], P(('dp', 'fsdp')), may hold values from -1.1953125 to 1.1953125
Outputs:
- output: bfloat16 [64, 512, 768], P('dp', 'fsdp')
- grad_tokens: bfloat16 [64, 512, 768], P('dp', 'fsdp')
- grad_qkv_weight: float32 [768, 2304], P(('dp', 'fsdp'))
- grad_out_weight: float32 [768, 768], P(('dp', 'fsdp'))
- grad_up_weight: float32 [768, 3072], P(('dp', 'fsdp'))
- grad_down_weight: float32 [3072, 768], P(('dp', 'fsdp'))
- grad_query_bias: float32 [768], P(('dp', 'fsdp'))
- grad_value_bias: float32 [768], P(('dp', 'fsdp'))
- grad_out_bias: float32 [768], P(('dp', 'fsdp'))
- grad_up_bias: float32 [3072], P(('dp', 'fsdp'))
- grad_down_bias: float32 [768], P(('dp', 'fsdp'))
- grad_attn_gain: float32 [768], P(('dp', 'fsdp'))
- grad_attn_shift: float32 [768], P(('dp', 'fsdp'))
- grad_ffn_gain: float32 [768], P(('dp', 'fsdp'))
- grad_ffn_shift: float32 [768], P(('dp', 'fsdp'))
Inputs may be any that keep to these rules, and one draw needn't show every extreme that they name: `key_mask`: positions 0 and 256 of every sequence are 1. `seq_lengths`: entry d * 2 + m is the length of the sequence dealt to micro-batch m of the device with index d over dp+fsdp. In each aligned block of 16 entries one is 512. `block_pattern`: both values occur. `deal_order`: each row holds each number once.
All inputs are finite; a program needn't handle non-finite values.
Results may differ from a plain program's by a relative error of at most 0.015.
Values may be sent and summed in bfloat16 or wider, within the bound.
No kernel may reach another device: no remote copies, remote signals or barrier semaphores. Data moves between devices by JAX's collectives and lax.ppermute only.
A program may use at most 192 MiB of HBM per device.

v0:
```python
import jax
import jax.numpy as jnp
from jax import lax
from jax.sharding import PartitionSpec as P

H = 12
HD = 64


EPSILON = 1e-12
NEGATIVE = -1e30


def layer_norm(residual, scales, offset):
    centre = residual - jnp.mean(residual, axis=-1, keepdims=True)
    spread = jnp.mean(centre * centre, axis=-1, keepdims=True)
    return centre * lax.rsqrt(spread + EPSILON) * scales + offset


def gelu_exact(upward):
    return jax.nn.gelu(upward, approximate=False)


def pair_blocks(blocks, pattern):
    swapped = (pattern == 1)[None, None, :, None]
    return jnp.where(swapped, blocks[::-1], blocks)


def key_masks(valid_row, pattern):
    blocks = valid_row.reshape(2, -1)
    swapped = (pattern == 1)[None, :, None]
    paired = jnp.where(swapped, blocks[::-1][:, None, :], blocks[:, None, :])
    return paired[:, :, None, :]


def over_rows(former, latter):
    return lax.dot_general(
        former, latter, (((0,), (0,)), ((), ())), preferred_element_type=jnp.float32
    )


def by_transpose(former, latter):
    return lax.dot_general(
        former, latter, (((1,), (1,)), ((), ())), preferred_element_type=jnp.float32
    )


def split_heads(project, model_width):
    half_len = project.shape[0] // 2
    queries = project[:, :model_width].reshape(2, half_len, H, HD)
    key_rows = project[:, model_width : 2 * model_width].reshape(2, half_len, H, HD)
    values = project[:, 2 * model_width :].reshape(2, half_len, H, HD)
    return (queries, key_rows, values)


def masked_scores(queries, keys_pair, key_valid):
    plain_scores = jnp.einsum(
        "bqhd,bkhd->bhqk", queries, keys_pair, preferred_element_type=jnp.float32
    ) * HD ** (-0.5)
    return jnp.where(key_valid, plain_scores, NEGATIVE)


def fetch_layer(shards):
    return (
        lax.all_gather(shards[0], ("dp", "fsdp"), axis=0, tiled=True),
        lax.all_gather(shards[1], ("dp", "fsdp"), axis=0, tiled=True),
        lax.all_gather(shards[2], ("dp", "fsdp"), axis=0, tiled=True),
        lax.all_gather(shards[3], ("dp", "fsdp"), axis=0, tiled=True),
        lax.all_gather(shards[4], ("dp", "fsdp"), axis=0, tiled=True),
        lax.all_gather(shards[5], ("dp", "fsdp"), axis=0, tiled=True),
        lax.all_gather(shards[6], ("dp", "fsdp"), axis=0, tiled=True),
        lax.all_gather(shards[7], ("dp", "fsdp"), axis=0, tiled=True),
        lax.all_gather(shards[8], ("dp", "fsdp"), axis=0, tiled=True),
        lax.all_gather(shards[9], ("dp", "fsdp"), axis=0, tiled=True),
        lax.all_gather(shards[10], ("dp", "fsdp"), axis=0, tiled=True),
        lax.all_gather(shards[11], ("dp", "fsdp"), axis=0, tiled=True),
        lax.all_gather(shards[12], ("dp", "fsdp"), axis=0, tiled=True),
    )


def layer_forward(weights, tokens_row, key_valid, pattern):
    (
        qkv_weight,
        out_weight,
        up_weight,
        down_weight,
        query_bias,
        value_bias,
        out_bias,
        up_bias,
        down_bias,
        attn_gain,
        attn_shift,
        ffn_gain,
        ffn_shift,
    ) = weights
    length_all = tokens_row.shape[0]
    model_width = out_weight.shape[0]
    bias_all = jnp.concatenate([query_bias, jnp.zeros_like(query_bias), value_bias]).astype(
        jnp.float32
    )
    project = (
        jnp.dot(tokens_row, qkv_weight, preferred_element_type=jnp.float32) + bias_all
    ).astype(jnp.bfloat16)
    queries, key_rows, values = split_heads(project, model_width)
    keys_pair = pair_blocks(key_rows, pattern)
    values_pair = pair_blocks(values, pattern)
    scores = masked_scores(queries, keys_pair, key_valid)
    row_top = jnp.max(scores, axis=-1, keepdims=True)
    exp_scores = jnp.exp(scores - row_top)
    row_total = jnp.sum(exp_scores, axis=-1, keepdims=True)
    attn_probs = exp_scores / row_total
    log_total = row_top + jnp.log(row_total)
    mixed_heads = jnp.einsum(
        "bhqk,bkhd->bqhd",
        attn_probs.astype(jnp.bfloat16),
        values_pair,
        preferred_element_type=jnp.float32,
    )
    mixed_heads = mixed_heads.reshape(length_all, model_width).astype(jnp.bfloat16)
    branch = jnp.dot(mixed_heads, out_weight, preferred_element_type=jnp.float32) + out_bias.astype(
        jnp.float32
    )
    resid_one = tokens_row.astype(jnp.float32) + branch
    hidden = layer_norm(resid_one, attn_gain.astype(jnp.float32), attn_shift.astype(jnp.float32))
    hidden_low = hidden.astype(jnp.bfloat16)
    upward = jnp.dot(hidden_low, up_weight, preferred_element_type=jnp.float32) + up_bias.astype(
        jnp.float32
    )
    active = gelu_exact(upward).astype(jnp.bfloat16)
    resid_two = hidden + (
        jnp.dot(active, down_weight, preferred_element_type=jnp.float32)
        + down_bias.astype(jnp.float32)
    )
    output_row = layer_norm(resid_two, ffn_gain.astype(jnp.float32), ffn_shift.astype(jnp.float32))
    stored = (project, log_total, mixed_heads, resid_one, hidden_low, upward, active, resid_two)
    return (output_row, stored)


def layer_backward(weights, tokens_row, key_valid, pattern, stored, upstream):
    (
        qkv_weight,
        out_weight,
        up_weight,
        down_weight,
        query_bias,
        value_bias,
        out_bias,
        up_bias,
        down_bias,
        attn_gain,
        attn_shift,
        ffn_gain,
        ffn_shift,
    ) = weights
    project, log_total, mixed_heads, resid_one, hidden_low, upward, active, resid_two = stored
    length_all = tokens_row.shape[0]
    model_width = out_weight.shape[0]
    unused, ffn_back = jax.vjp(
        layer_norm, resid_two, ffn_gain.astype(jnp.float32), ffn_shift.astype(jnp.float32)
    )
    grad_two, grad_ffn_gain, grad_ffn_shift = ffn_back(upstream)
    down_low = grad_two.astype(jnp.bfloat16)
    grad_down_weight = over_rows(active, down_low)
    grad_down_bias = jnp.sum(down_low, axis=0, dtype=jnp.float32)
    unused, gelu_back = jax.vjp(gelu_exact, upward)
    (grad_upward,) = gelu_back(by_transpose(down_low, down_weight))
    up_low = grad_upward.astype(jnp.bfloat16)
    grad_up_weight = over_rows(hidden_low, up_low)
    grad_up_bias = jnp.sum(up_low, axis=0, dtype=jnp.float32)
    grad_hidden = grad_two + by_transpose(up_low, up_weight)
    unused, attn_back = jax.vjp(
        layer_norm, resid_one, attn_gain.astype(jnp.float32), attn_shift.astype(jnp.float32)
    )
    grad_one, grad_attn_gain, grad_attn_shift = attn_back(grad_hidden)
    out_low = grad_one.astype(jnp.bfloat16)
    grad_out_weight = over_rows(mixed_heads, out_low)
    grad_out_bias = jnp.sum(out_low, axis=0, dtype=jnp.float32)
    grad_mixed = (
        by_transpose(out_low, out_weight).astype(jnp.bfloat16).reshape(2, length_all // 2, H, HD)
    )
    queries, key_rows, values = split_heads(project, model_width)
    keys_pair = pair_blocks(key_rows, pattern)
    values_pair = pair_blocks(values, pattern)
    scores = masked_scores(queries, keys_pair, key_valid)
    attn_probs = jnp.exp(scores - log_total)
    grad_probs = jnp.einsum(
        "bqhd,bkhd->bhqk", grad_mixed, values_pair, preferred_element_type=jnp.float32
    )
    grad_values = pair_blocks(
        jnp.einsum(
            "bhqk,bqhd->bkhd",
            attn_probs.astype(jnp.bfloat16),
            grad_mixed,
            preferred_element_type=jnp.float32,
        ),
        pattern,
    )
    row_inner = jnp.sum(attn_probs * grad_probs, axis=-1, keepdims=True)
    grad_scores = (attn_probs * (grad_probs - row_inner)).astype(jnp.bfloat16)
    grad_queries = jnp.einsum(
        "bhqk,bkhd->bqhd", grad_scores, keys_pair, preferred_element_type=jnp.float32
    ) * HD ** (-0.5)
    grad_keys = pair_blocks(
        jnp.einsum("bhqk,bqhd->bkhd", grad_scores, queries, preferred_element_type=jnp.float32)
        * HD ** (-0.5),
        pattern,
    )
    grad_project = jnp.concatenate(
        [
            grad_queries.reshape(length_all, model_width),
            grad_keys.reshape(length_all, model_width),
            grad_values.reshape(length_all, model_width),
        ],
        axis=1,
    ).astype(jnp.bfloat16)
    grad_qkv_weight = over_rows(tokens_row, grad_project)
    grad_query_bias = jnp.sum(grad_project[:, :model_width], axis=0, dtype=jnp.float32)
    grad_value_bias = jnp.sum(grad_project[:, 2 * model_width :], axis=0, dtype=jnp.float32)
    grad_row = grad_one + by_transpose(grad_project, qkv_weight)
    weight_grads = (
        grad_qkv_weight,
        grad_out_weight,
        grad_up_weight,
        grad_down_weight,
        grad_query_bias,
        grad_value_bias,
        grad_out_bias,
        grad_up_bias,
        grad_down_bias,
        grad_attn_gain,
        grad_attn_shift,
        grad_ffn_gain,
        grad_ffn_shift,
    )
    return (grad_row, weight_grads)


def local(
    tokens,
    cotangent,
    key_mask,
    seq_lengths,
    block_pattern,
    deal_order,
    qkv_weight,
    out_weight,
    up_weight,
    down_weight,
    query_bias,
    value_bias,
    out_bias,
    up_bias,
    down_bias,
    attn_gain,
    attn_shift,
    ffn_gain,
    ffn_shift,
):
    shards = (
        qkv_weight,
        out_weight,
        up_weight,
        down_weight,
        query_bias,
        value_bias,
        out_bias,
        up_bias,
        down_bias,
        attn_gain,
        attn_shift,
        ffn_gain,
        ffn_shift,
    )
    fsdp_size = lax.axis_size("fsdp")
    micro_count = seq_lengths.shape[0]
    piece_len = tokens.shape[1]
    seq_len = piece_len * fsdp_size
    order_row = deal_order[0]
    positions = jnp.arange(seq_len, dtype=jnp.int32)
    output_parts = []
    grad_parts = []
    totals = None
    for micro_index in range(micro_count):
        chosen = order_row[micro_index * fsdp_size : (micro_index + 1) * fsdp_size]
        tokens_row, mask_row, upstream_row = (
            lax.all_to_all(
                jnp.take(tokens, chosen, axis=0), "fsdp", split_axis=0, concat_axis=1, tiled=True
            ),
            lax.all_to_all(
                jnp.take(key_mask, chosen, axis=0), "fsdp", split_axis=0, concat_axis=1, tiled=True
            ),
            lax.all_to_all(
                jnp.take(cotangent, chosen, axis=0), "fsdp", split_axis=0, concat_axis=1, tiled=True
            ),
        )
        weights = fetch_layer(shards)
        valid_row = (mask_row[0] == 1) & (positions < seq_lengths[micro_index])
        key_valid = key_masks(valid_row, block_pattern)
        output_row, stored = layer_forward(weights, tokens_row[0], key_valid, block_pattern)
        weights = (
            lax.all_gather(shards[0], ("dp", "fsdp"), axis=0, tiled=True),
            lax.all_gather(shards[1], ("dp", "fsdp"), axis=0, tiled=True),
            lax.all_gather(shards[2], ("dp", "fsdp"), axis=0, tiled=True),
            lax.all_gather(shards[3], ("dp", "fsdp"), axis=0, tiled=True),
            lax.all_gather(shards[4], ("dp", "fsdp"), axis=0, tiled=True),
            lax.all_gather(shards[5], ("dp", "fsdp"), axis=0, tiled=True),
            lax.all_gather(shards[6], ("dp", "fsdp"), axis=0, tiled=True),
            lax.all_gather(shards[7], ("dp", "fsdp"), axis=0, tiled=True),
            lax.all_gather(shards[8], ("dp", "fsdp"), axis=0, tiled=True),
            lax.all_gather(shards[9], ("dp", "fsdp"), axis=0, tiled=True),
            lax.all_gather(shards[10], ("dp", "fsdp"), axis=0, tiled=True),
            lax.all_gather(shards[11], ("dp", "fsdp"), axis=0, tiled=True),
            lax.all_gather(shards[12], ("dp", "fsdp"), axis=0, tiled=True),
        )
        unused, stored = layer_forward(weights, tokens_row[0], key_valid, block_pattern)
        grad_row, weight_grads = layer_backward(
            weights,
            tokens_row[0],
            key_valid,
            block_pattern,
            stored,
            upstream_row[0].astype(jnp.float32),
        )
        returned = (
            lax.all_to_all(
                output_row.astype(jnp.bfloat16)[None],
                "fsdp",
                split_axis=1,
                concat_axis=0,
                tiled=True,
            ),
            lax.all_to_all(
                grad_row.astype(jnp.bfloat16)[None], "fsdp", split_axis=1, concat_axis=0, tiled=True
            ),
        )
        output_parts.append(returned[0])
        grad_parts.append(returned[1])
        if totals is None:
            totals = weight_grads
        else:
            totals = tuple((earlier + current for earlier, current in zip(totals, weight_grads)))
    totals = lax.psum_scatter(totals, ("dp", "fsdp"), scatter_dimension=0, tiled=True)
    slot_ids = jnp.arange(order_row.shape[0], dtype=jnp.int32)
    inverse = jnp.sum(
        jnp.where(order_row[:, None] == slot_ids[None, :], slot_ids[:, None], 0), axis=0
    )
    output_given = jnp.take(jnp.concatenate(output_parts, axis=0), inverse, axis=0)
    grad_given = jnp.take(jnp.concatenate(grad_parts, axis=0), inverse, axis=0)
    return (
        output_given,
        grad_given,
        totals[0],
        totals[1],
        totals[2],
        totals[3],
        totals[4],
        totals[5],
        totals[6],
        totals[7],
        totals[8],
        totals[9],
        totals[10],
        totals[11],
        totals[12],
    )


def solution(mesh):
    in_specs = (
        P("dp", "fsdp", None),
        P("dp", "fsdp", None),
        P("dp", "fsdp"),
        P(("dp", "fsdp")),
        P(),
        P("dp", None),
        P(("dp", "fsdp"), None),
        P(("dp", "fsdp"), None),
        P(("dp", "fsdp"), None),
        P(("dp", "fsdp"), None),
        P(("dp", "fsdp")),
        P(("dp", "fsdp")),
        P(("dp", "fsdp")),
        P(("dp", "fsdp")),
        P(("dp", "fsdp")),
        P(("dp", "fsdp")),
        P(("dp", "fsdp")),
        P(("dp", "fsdp")),
        P(("dp", "fsdp")),
    )
    out_specs = (
        P("dp", "fsdp", None),
        P("dp", "fsdp", None),
        P(("dp", "fsdp"), None),
        P(("dp", "fsdp"), None),
        P(("dp", "fsdp"), None),
        P(("dp", "fsdp"), None),
        P(("dp", "fsdp")),
        P(("dp", "fsdp")),
        P(("dp", "fsdp")),
        P(("dp", "fsdp")),
        P(("dp", "fsdp")),
        P(("dp", "fsdp")),
        P(("dp", "fsdp")),
        P(("dp", "fsdp")),
        P(("dp", "fsdp")),
    )
    return jax.shard_map(local, mesh=mesh, in_specs=in_specs, out_specs=out_specs, check_vma=False)
```

profile of v0, /device:TPU:0, one launch (start us, length us, event | category | flops | bytes accessed | tf_op | source)
XLA Modules:
  0.0 894.9 jit_solution(14152277786469803366)
XLA Ops:
  12.2 5.2 all-to-all-start.1
  30.1 41.7 %all-reduce.19 = (bf16[768]{0:T(1024)(128)(2,1)S(1)}, bf16[768]{0:T(1024)(128)(2,1)S(1)}, bf16[768]{0:T(1024)(128)(2,1)S(1)}, bf16[768]{0:T(1024)(128)(2,1)S(1)}...) all-reduce(bf16[768]{0:T(1024)(128)(2,1)S(1)} %dynamic-update-slice, ...), channel_id=1, replica_groups=mesh['dp'=4,'fsdp'=8] {'dp','fsdp'}, use_global_device_ids=true, to_apply=%add.1 | all-reduce | flops 9216 | bytes 36864
  87.1 10.8 %all-to-all-done = bf16[8,64,768]{2,1,0:T(8,128)(2,1)S(1)} async-done(((bf16[8,64,768]{2,1,0:T(8,128)(2,1)}), bf16[8,64,768]{2,1,0:T(8,128)(2,1)S(1)}, u32[]{:S(2)}, u32[]{:S(2)}) %all-to-all-start) | async-done | bytes 786464 | tf_op jit(solution)/shard_map/all_to_all | solution.py:287
  135.0 4.8 reverse_select_fusion.4
  163.5 37.2 %all-gather.9.cloned.1.call-done = bf16[768,3072]{1,0:T(8,128)(2,1)} async-done(((bf16[24,3072]{1,0:T(8,128)(2,1)}), bf16[768,3072]{1,0:T(8,128)(2,1)}) %all-gather.9.cloned.1.call-update) | async-done | bytes 4718608 | tf_op jit(solution)/shard_map/all_gather | solution.py:67
  200.7 4.8 fusion.69
  208.2 34.9 %multiply_convert_fusion.3 = (bf16[512,3072]{1,0:T(8,128)(2,1)}, f32[512,3072]{1,0:T(8,128)}, bf16[512,3072]{1,0:T(8,128)(2,1)}, f32[512,3072]{1,0:T(8,128)}, f32[512,3072]{1,0:T(8,128)}) fusion(f32[3072]{0:T(1024)S(1)} %convert_element_type.223, f32[512,3072]{1,0:T(8,128)S(1)} %fusion.69, bf16[768,3072]{1,0:T(8,128)(2,1)S(1)} %copy-done.62, ...), kind=kOutput, calls=%fused_computation.38 | convolution fusion | flops 2625503232 | bytes 37771264 | tf_op jit(solution)/shard_map/dot_general | solution.py:127
  243.2 22.7 %all-gather.11.cloned.1.call-done = bf16[3072,768]{1,0:T(8,128)(2,1)} async-done(((bf16[96,768]{1,0:T(8,128)(2,1)}), bf16[3072,768]{1,0:T(8,128)(2,1)}) %all-gather.11.cloned.1.call-update) | async-done | bytes 4718608 | tf_op jit(solution)/shard_map/all_gather | solution.py:68
  265.9 6.6 fusion.88
  282.7 10.5 %all-to-all-done.6 = bf16[8,64,768]{2,1,0:T(8,128)(2,1)} async-done(((bf16[8,64,768]{2,1,0:T(8,128)(2,1)}), bf16[8,64,768]{2,1,0:T(8,128)(2,1)}, u32[]{:S(2)}, u32[]{:S(2)}) %all-to-all-start.6) | async-done | bytes 786464 | tf_op jit(solution)/shard_map/all_to_all | solution.py:293
  306.6 17.6 %convert_reduce_fusion.1 = (f32[3072]{0:T(1024)S(1)}, bf16[512,3072]{1,0:T(8,128)(2,1)}, f32[3072]{0:T(1024)S(1)}, bf16[512,3072]{1,0:T(8,128)(2,1)}) fusion(f32[512,3072]{1,0:T(8,128)} %get-tuple-element.67, f32[512,3072]{1,0:T(8,128)} %get-tuple-element.124, f32[3072]{0:T(1024)S(1)} %convert_element_type.223, f32[512,3072]{1,0:T(8,128)} %fusion.90, ...), kind=kOutput, calls=%fused_computation.13 | convolution fusion | flops 2469390336 | bytes 43290624 | tf_op jit(solution)/shard_map/dot_general | solution.py:43
  324.3 6.1 add_add_fusion.8
  330.4 5.8 multiply_reduce_fusion.3
  342.4 4.9 fusion.36
  363.0 4.8 fusion.39
  367.8 7.0 multiply_reduce_fusion
  377.5 6.4 multiply_convert_fusion
  397.4 5.0 convolution_add_fusion
  402.4 5.5 fusion.71
  407.9 5.9 convolution_add_fusion.2
  414.9 4.8 fusion.93
  419.7 5.3 convolution_add_fusion.1
  427.9 6.3 reduce.12
  444.3 6.3 reduce.13
  460.0 4.8 fusion.48
  466.0 6.3 reduce.11
  481.1 4.8 fusion.49
  488.2 7.5 reduce.10
  505.2 42.9 %all-reduce.18 = (f32[768]{0:T(1024)S(1)}, f32[768]{0:T(1024)S(1)}, f32[768]{0:T(1024)S(1)}, f32[3072]{0:T(1024)S(1)}, f32[768]{0:T(1024)S(1)}, /*index=5*/f32[7...) all-reduce(f32[768]{0:T(1024)S(1)} %add.335, ...), channel_id=6, replica_groups=mesh['dp'=4,'fsdp'=8] {'dp','fsdp'}, use_global_device_ids=true, to_apply=%region_29.33.clone | all-reduce | flops 9216 | bytes 73728
  581.1 23.3 %reduce-scatter.5.cloned.1.call-done = f32[24,2304]{1,0:T(8,128)} async-done(((f32[768,2304]{1,0:T(8,128)}), f32[24,2304]{1,0:T(8,128)}) %reduce-scatter.5.cloned.1.call-update) | async-done | bytes 221200 | tf_op jit(solution)/shard_map/reduce_scatter | solution.py:343
  604.5 141.2 %reduce-scatter.9.cloned.1.call-done = f32[24,3072]{1,0:T(8,128)} async-done(((f32[768,3072]{1,0:T(8,128)}), f32[24,3072]{1,0:T(8,128)}) %reduce-scatter.9.cloned.1.call-update) | async-done | bytes 294928 | tf_op jit(solution)/shard_map/reduce_scatter | solution.py:343
  745.7 142.1 %reduce-scatter.11.cloned.1.call-done = f32[96,768]{1,0:T(8,128)} async-done(((f32[3072,768]{1,0:T(8,128)}), f32[96,768]{1,0:T(8,128)}) %reduce-scatter.11.cloned.1.call-update) | async-done | bytes 294928 | tf_op jit(solution)/shard_map/reduce_scatter | solution.py:343
  (402 shorter events, 235.0 us)
Async XLA Ops:
  7.2 12.0 %copy-start = (bf16[16,64,768]{2,1,0:T(8,128)(2,1)S(1)}, bf16[16,64,768]{2,1,0:T(8,128)(2,1)}, u32[]{:S(2)}) copy-start(bf16[16,64,768]{2,1,0:T(8,128)(2,1)} %param.26) | copy-start | bytes 4718596
  7.2 94.3 %all-gather.5.cloned.1.call-start = ((), (), s32[]{:S(2)}) async-start(), calls=%async_computation.14 | async-start | bytes 3649536 | tf_op jit(solution)/shard_map/all_gather | solution.py:65
  7.9 140.5 %all-gather.7.cloned.1.call-start = ((), (), s32[]{:S(2)}) async-start(), calls=%async_computation.15 | async-start | bytes 1216512 | tf_op jit(solution)/shard_map/all_gather | solution.py:66
  8.7 192.0 %all-gather.9.cloned.1.call-start = ((), (), s32[]{:S(2)}) async-start(), calls=%async_computation.16 | async-start | bytes 4866048 | tf_op jit(solution)/shard_map/all_gather | solution.py:67
  12.2 61.5 %all-to-all-start.1 = ((s32[8,1,64]{2,1,0:T(1,128)}), s32[8,1,64]{2,1,0:T(1,128)S(1)}, u32[]{:S(2)}, u32[]{:S(2)}) async-start(s32[8,1,64]{2,1,0:T(1,128)} %bitcast.4), calls=%async_computation.1 | async-start | bytes 8192 | tf_op jit(solution)/shard_map/all_to_all | solution.py:290
  17.3 248.6 %all-gather.11.cloned.1.call-start = ((), (), s32[]{:S(2)}) async-start(), calls=%async_computation.17 | async-start | bytes 4866048 | tf_op jit(solution)/shard_map/all_gather | solution.py:68
  24.6 110.4 %copy-start.58 = (pred[12]{0:T(512)(128)(4,1)}, pred[12]{0:T(512)(128)(4,1)S(1)}, u32[]{:S(2)}) copy-start(pred[12]{0:T(512)(128)(4,1)S(1)} %broadcast_compare_fusion) | copy-start | bytes 40
  27.2 44.6 %copy-start.61 = (s32[2]{0:T(128)S(1)}, s32[2]{0:T(128)}, u32[]{:S(2)}) copy-start(s32[2]{0:T(128)} %param.28) | copy-start | bytes 28
  73.6 8.2 all-to-all-start.4
  81.8 16.1 %all-to-all-start = ((bf16[8,64,768]{2,1,0:T(8,128)(2,1)}), bf16[8,64,768]{2,1,0:T(8,128)(2,1)S(1)}, u32[]{:S(2)}, u32[]{:S(2)}) async-start(bf16[8,64,768]{2,1,0:T(8,128)(2,1)} %get-tuple-element.103), calls=%async_computation | async-start | bytes 1572864 | tf_op jit(solution)/shard_map/all_to_all | solution.py:287
  97.9 18.0 %all-to-all-start.3 = ((bf16[8,64,768]{2,1,0:T(8,128)(2,1)}), bf16[8,64,768]{2,1,0:T(8,128)(2,1)S(1)}, u32[]{:S(2)}, u32[]{:S(2)}) async-start(bf16[8,64,768]{2,1,0:T(8,128)(2,1)} %get-tuple-element.105), calls=%async_computation.3 | async-start | bytes 1572864 | tf_op jit(solution)/shard_map/all_to_all | solution.py:287
  110.0 29.9 %copy-start.15 = (bf16[2,256,12,64]{1,0,3,2:T(2,128)(2,1)}, bf16[2,256,12,64]{1,0,3,2:T(2,128)(2,1)S(1)}, u32[]{:S(2)}) copy-start(bf16[2,256,12,64]{1,0,3,2:T(2,128)(2,1)S(1)} %reshape.373) | copy-start | bytes 2359300
  115.9 160.5 %all-to-all-start.8 = ((bf16[8,64,768]{2,1,0:T(8,128)(2,1)}), bf16[8,64,768]{2,1,0:T(8,128)(2,1)}, u32[]{:S(2)}, u32[]{:S(2)}) async-start(bf16[8,64,768]{2,1,0:T(8,128)(2,1)} %get-tuple-element.104), calls=%async_computation.8 | async-start | bytes 1572864 | tf_op jit(solution)/shard_map/all_to_all | solution.py:293
  129.9 22.1 %copy-start.13 = (bf16[2,256,12,64]{1,0,3,2:T(2,128)(2,1)}, bf16[2,256,12,64]{1,0,3,2:T(2,128)(2,1)S(1)}, u32[]{:S(2)}) copy-start(bf16[2,256,12,64]{1,0,3,2:T(2,128)(2,1)S(1)} %reshape.376) | copy-start | bytes 2359300
  139.8 12.2 %copy-start.6 = (bf16[2,256,12,64]{1,3,2,0:T(8,128)(2,1)}, bf16[2,256,12,64]{1,3,2,0:T(8,128)(2,1)S(1)}, u32[]{:S(2)}) copy-start(bf16[2,256,12,64]{1,3,2,0:T(8,128)(2,1)S(1)} %get-tuple-element.108) | copy-start | bytes 2359300
  163.5 44.8 %copy-start.21 = (f32[512,768]{1,0:T(8,128)S(1)}, f32[512,768]{1,0:T(8,128)}, u32[]{:S(2)}) copy-start(f32[512,768]{1,0:T(8,128)} %copy-done.20) | copy-start | bytes 4718596
  276.4 16.9 %copy-start.54 = (f32[768]{0:T(1024)S(1)}, f32[768]{0:T(1024)}, u32[]{:S(2)}) copy-start(f32[768]{0:T(1024)} %convert_element_type.226) | copy-start | bytes 9220
  276.4 16.9 %all-to-all-start.6 = ((bf16[8,64,768]{2,1,0:T(8,128)(2,1)}), bf16[8,64,768]{2,1,0:T(8,128)(2,1)}, u32[]{:S(2)}, u32[]{:S(2)}) async-start(bf16[8,64,768]{2,1,0:T(8,128)(2,1)} %get-tuple-element.102), calls=%async_computation.6 | async-start | bytes 1572864 | tf_op jit(solution)/shard_map/all_to_all | solution.py:293
  280.6 300.5 %reduce-scatter.7.cloned.1.call-start = ((), (), s32[]{:S(2)}) async-start(), calls=%async_computation.19 | async-start | bytes 2433024 | tf_op jit(solution)/shard_map/reduce_scatter | solution.py:343
  281.0 15.5 %copy-start.57 = (f32[768]{0:T(1024)S(1)}, f32[768]{0:T(1024)}, u32[]{:S(2)}) copy-start(f32[768]{0:T(1024)} %convert_element_type.227) | copy-start | bytes 9220
  306.6 17.7 %copy-start.28 = (f32[512,768]{1,0:T(8,128)S(1)}, f32[512,768]{1,0:T(8,128)}, u32[]{:S(2)}) copy-start(f32[512,768]{1,0:T(8,128)} %copy-done.27) | copy-start | bytes 4718596
  342.4 9.4 %slice-start = ((s8[6291456]{0:T(1024)(128)(4,1)}), s8[4194304]{0:T(1024)(128)(4,1)S(1)}, s32[]{:S(2)}) async-start(s8[6291456]{0:T(1024)(128)(4,1)} %bitcast.201), calls=%async_computation.22 | async-start | bytes 8388608
  377.0 227.5 %reduce-scatter.5.cloned.1.call-start = ((), (), s32[]{:S(2)}) async-start(), calls=%async_computation.18 | async-start | bytes 7299072 | tf_op jit(solution)/shard_map/reduce_scatter | solution.py:343
  402.4 343.3 %reduce-scatter.9.cloned.1.call-start = ((), (), s32[]{:S(2)}) async-start(), calls=%async_computation.20 | async-start | bytes 9732096 | tf_op jit(solution)/shard_map/reduce_scatter | solution.py:343
  413.8 474.0 %reduce-scatter.11.cloned.1.call-start = ((), (), s32[]{:S(2)}) async-start(), calls=%async_computation.21 | async-start | bytes 9732096 | tf_op jit(solution)/shard_map/reduce_scatter | solution.py:343
  427.4 14.4 %copy-start.60 = (s32[1,16]{1,0:T(1,128)S(1)}, s32[1,16]{1,0:T(1,128)}, u32[]{:S(2)}) copy-start(s32[1,16]{1,0:T(1,128)} %param.30) | copy-start | bytes 196
  437.2 18.4 %all-to-all-start.5 = ((bf16[8,2,24576]{2,1,0:T(2,128)(2,1)}), bf16[8,2,24576]{2,1,0:T(2,128)(2,1)}, u32[]{:S(2)}, u32[]{:S(2)}) async-start(bf16[8,2,24576]{2,1,0:T(2,128)(2,1)} %reshape.496), calls=%async_computation.5 | async-start | bytes 1572864 | tf_op jit(solution)/shard_map/all_to_all | solution.py:326
  455.6 19.8 %all-to-all-start.2 = ((bf16[8,2,24576]{2,1,0:T(2,128)(2,1)}), bf16[8,2,24576]{2,1,0:T(2,128)(2,1)}, u32[]{:S(2)}, u32[]{:S(2)}) async-start(bf16[8,2,24576]{2,1,0:T(2,128)(2,1)} %reshape.498), calls=%async_computation.2 | async-start | bytes 1572864 | tf_op jit(solution)/shard_map/all_to_all | solution.py:326
  475.4 23.4 %all-to-all-start.7 = ((bf16[8,2,24576]{2,1,0:T(2,128)(2,1)}), bf16[8,2,24576]{2,1,0:T(2,128)(2,1)}, u32[]{:S(2)}, u32[]{:S(2)}) async-start(bf16[8,2,24576]{2,1,0:T(2,128)(2,1)} %reshape.502), calls=%async_computation.7 | async-start | bytes 1572864 | tf_op jit(solution)/shard_map/all_to_all | solution.py:333
  488.2 16.3 %copy-start.10 = (bf16[96,8,2,256]{3,1,2,0:T(8,128)(2,1)S(1)}, bf16[96,8,2,256]{3,1,2,0:T(8,128)(2,1)}, u32[]{:S(2)}) copy-start(bf16[96,8,2,256]{3,1,2,0:T(8,128)(2,1)} %copy-done.9) | copy-start | bytes 2359300
  498.8 68.1 %all-to-all-start.9 = ((bf16[8,2,24576]{2,1,0:T(2,128)(2,1)}), bf16[8,2,24576]{2,1,0:T(2,128)(2,1)}, u32[]{:S(2)}, u32[]{:S(2)}) async-start(bf16[8,2,24576]{2,1,0:T(2,128)(2,1)} %reshape.500), calls=%async_computation.9 | async-start | bytes 1572864 | tf_op jit(solution)/shard_map/all_to_all | solution.py:333
  575.4 312.4 %copy-start.1 = (bf16[16,64,768]{2,1,0:T(8,128)(2,1)S(1)}, bf16[16,64,768]{2,1,0:T(8,128)(2,1)}, u32[]{:S(2)}) copy-start(bf16[16,64,768]{2,1,0:T(8,128)(2,1)} %param.26) | copy-start | bytes 4718596
  (69 other events, 304.3 us)
Sparse Core Ops, SparseCore 0:
  10.9 63.0 all-gather.4
  76.9 55.9 all-gather.6
  135.8 64.8 all-gather.8
  203.4 62.4 all-gather.10
  377.1 101.1 reduce-scatter.6
  485.4 119.0 reduce-scatter.4
  611.0 134.6 reduce-scatter.8
  753.2 134.5 reduce-scatter.10
where the time goes:
time: 905 us; the launch traced here: 895 us
  waiting for transfers between devices  397 us (44%)
  matrix products  178 us (20%)
  local copies, waits for them, and re-layouts  102 us (11%)
  blocking collectives  84.6 us (9%)
  other arithmetic  74.1 us (8%)
  starting transfers between devices  43.1 us (5%)
  between operations  16.2 us (2%)
    reduce_scatter x4, waiting for transfers between devices, local(): lax.psum_scatter(totals, ('dp', 'fsdp'), scatter_dimension=0, tiled=True)  307 us
    unnamed x2, blocking collectives  84.6 us
    unnamed x219, local copies, waits for them, and re-layouts  50.2 us
    dot_general x8, matrix products, by_transpose(): lax.dot_general(former, latter, (((1,), (1,)), ((), ())), preferred_eleme...  45.3 us
    dot_general x2, matrix products, layer_forward(): jnp.dot(hidden_low, up_weight, preferred_element_type=jnp.float32)  39.8 us
    all_gather x1, waiting for transfers between devices, fetch_layer(): lax.all_gather(shards[2], ('dp', 'fsdp'), axis=0, tiled=True)  37.2 us
    dot_general x8, matrix products, over_rows(): lax.dot_general(former, latter, (((0,), (0,)), ((), ())), preferred_eleme...  33 us
    unnamed x6, other arithmetic  26.4 us
  transfers between devices with their start and end apart: 18, of which 9 were waited for; matrix products, arithmetic and copies ran while one was open for 29% of the time, Pallas kernels for 0%

commit v1 on v0

v1 whole, which is shorter than its diff:
```python
import functools

import jax
import jax.numpy as jnp
from jax import lax
from jax.experimental import pallas as pl
from jax.experimental.pallas import tpu as pltpu
from jax.sharding import PartitionSpec as P

H = 12
HD = 64
EPSILON = 1e-12
NEGATIVE = -1e30
BF = jnp.bfloat16
F32 = jnp.float32
VMEM_LIMIT = 56 * 1024 * 1024
BOTH = ("dp", "fsdp")


def dot(a, b):
    return jnp.dot(a, b, preferred_element_type=F32)


def dot_nt(a, b):
    return lax.dot_general(a, b, (((1,), (1,)), ((), ())), preferred_element_type=F32)


def dot_tn(a, b):
    return lax.dot_general(a, b, (((0,), (0,)), ((), ())), preferred_element_type=F32)


def attention_fwd_kernel(heads, pattern, q_ref, k_ref, v_ref, valid_ref, mixed_ref, probs_ref):
    first = pl.program_id(1) * heads
    half = q_ref.shape[1] // 2
    for h in range(heads):
        pat = pattern[first + h]
        cols = slice(h * HD, (h + 1) * HD)
        for b in range(2):
            met = jnp.where(pat == 1, 1 - b, b)
            off = pl.multiple_of(met * half, half)
            q = q_ref[0, b * half : (b + 1) * half, cols] * jnp.asarray(HD ** (-0.5), BF)
            k = k_ref[0, pl.ds(off, half), cols]
            v = v_ref[0, pl.ds(off, half), cols]
            ok = valid_ref[0, met]
            scores = jnp.where(ok > 0.0, dot_nt(q, k), NEGATIVE)
            top = jnp.max(scores, axis=-1, keepdims=True)
            e = jnp.exp(scores - top)
            p = (e / jnp.sum(e, axis=-1, keepdims=True)).astype(BF)
            probs_ref[0, h, b] = p
            mixed_ref[0, b * half : (b + 1) * half, cols] = dot(p, v).astype(BF)


def attention_fwd(project, valid, pattern, heads=4):
    n, length, width3 = project.shape
    width = width3 // 3
    half = length // 2
    steps = H // heads
    wide = heads * HD

    def part(which):
        return pl.BlockSpec((1, length, wide), lambda s, g, pat: (s, 0, which * steps + g))

    return pl.pallas_call(
        functools.partial(attention_fwd_kernel, heads),
        grid_spec=pltpu.PrefetchScalarGridSpec(
            num_scalar_prefetch=1,
            grid=(n, steps),
            in_specs=[part(0), part(1), part(2), pl.BlockSpec((1, 2, 1, half), lambda s, g, pat: (s, 0, 0, 0))],
            out_specs=[
                pl.BlockSpec((1, length, wide), lambda s, g, pat: (s, 0, g)),
                pl.BlockSpec((1, heads, 2, half, half), lambda s, g, pat: (s, g, 0, 0, 0)),
            ],
        ),
        out_shape=[
            jax.ShapeDtypeStruct((n, length, width), BF),
            jax.ShapeDtypeStruct((n, H, 2, half, half), BF),
        ],
        compiler_params=pltpu.CompilerParams(vmem_limit_bytes=VMEM_LIMIT),
        cost_estimate=pl.CostEstimate(
            flops=4 * n * H * 2 * half * half * HD * 4, bytes_accessed=12_000_000, transcendentals=n * H * 2 * half * half
        ),
        name="attention_fwd",
    )(pattern, project, project, project, valid)


def attention_bwd_kernel(heads, pattern, q_ref, k_ref, v_ref, probs_ref, g_ref, dq_ref, dk_ref, dv_ref):
    first = pl.program_id(1) * heads
    half = q_ref.shape[1] // 2
    scale = HD ** (-0.5)
    for h in range(heads):
        pat = pattern[first + h]
        cols = slice(h * HD, (h + 1) * HD)
        for b in range(2):
            met = jnp.where(pat == 1, 1 - b, b)
            off = pl.multiple_of(met * half, half)
            rows = slice(b * half, (b + 1) * half)
            q = q_ref[0, rows, cols]
            g = g_ref[0, rows, cols]
            k = k_ref[0, pl.ds(off, half), cols]
            v = v_ref[0, pl.ds(off, half), cols]
            p = probs_ref[0, h, b]
            wide = p.astype(F32)
            gp = dot_nt(g, v)
            inner = jnp.sum(wide * gp, axis=-1, keepdims=True)
            gs = (wide * (gp - inner)).astype(BF)
            dq_ref[0, rows, cols] = (dot(gs, k) * scale).astype(BF)
            dk_ref[0, pl.ds(off, half), cols] = (dot_tn(gs, q) * scale).astype(BF)
            dv_ref[0, pl.ds(off, half), cols] = dot_tn(p, g).astype(BF)


def attention_bwd(project, probs, grad_mixed, pattern, heads=4):
    n, length, width3 = project.shape
    width = width3 // 3
    half = length // 2
    steps = H // heads
    wide = heads * HD

    def part(which):
        return pl.BlockSpec((1, length, wide), lambda s, g, pat: (s, 0, which * steps + g))

    out = pl.BlockSpec((1, length, wide), lambda s, g, pat: (s, 0, g))
    return pl.pallas_call(
        functools.partial(attention_bwd_kernel, heads),
        grid_spec=pltpu.PrefetchScalarGridSpec(
            num_scalar_prefetch=1,
            grid=(n, steps),
            in_specs=[
                part(0),
                part(1),
                part(2),
                pl.BlockSpec((1, heads, 2, half, half), lambda s, g, pat: (s, g, 0, 0, 0)),
                out,
            ],
            out_specs=[out, out, out],
        ),
        out_shape=[jax.ShapeDtypeStruct((n, length, width), BF)] * 3,
        compiler_params=pltpu.CompilerParams(vmem_limit_bytes=VMEM_LIMIT),
        cost_estimate=pl.CostEstimate(
            flops=8 * n * H * 2 * half * half * HD * 4, bytes_accessed=16_000_000, transcendentals=0
        ),
        name="attention_bwd",
    )(pattern, project, project, project, probs, grad_mixed)


def ffn_up_kernel(chunk, h_ref, w_ref, b_ref, act_ref, slope_ref):
    h = h_ref[...]
    for start in range(0, w_ref.shape[1], chunk):
        cols = slice(start, start + chunk)
        u = dot(h, w_ref[:, cols]) + b_ref[:, cols]
        phi = 0.5 + 0.5 * lax.erf(u * (2.0 ** -0.5))
        density = jnp.exp(-0.5 * u * u) * 0.3989422804014327
        act_ref[:, cols] = (u * phi).astype(BF)
        slope_ref[:, cols] = (phi + u * density).astype(BF)


def ffn_up(hidden_low, weight, bias, tile=256, chunk=512):
    rows, width = hidden_low.shape
    wide = weight.shape[1]
    out = pl.BlockSpec((tile, wide), lambda i: (i, 0))
    return pl.pallas_call(
        functools.partial(ffn_up_kernel, chunk),
        grid=(rows // tile,),
        in_specs=[
            pl.BlockSpec((tile, width), lambda i: (i, 0)),
            pl.BlockSpec((width, wide), lambda i: (0, 0)),
            pl.BlockSpec((1, wide), lambda i: (0, 0)),
        ],
        out_specs=[out, out],
        out_shape=[jax.ShapeDtypeStruct((rows, wide), BF)] * 2,
        compiler_params=pltpu.CompilerParams(vmem_limit_bytes=VMEM_LIMIT),
        cost_estimate=pl.CostEstimate(
            flops=2 * rows * width * wide + 40 * rows * wide, bytes_accessed=20_000_000, transcendentals=rows * wide
        ),
        name="ffn_up",
    )(hidden_low, weight, bias)


def plane_groups(size):
    return [list(range(c, size, 2)) for c in range(2)]


def core_swap(a):
    return lax.ppermute(a, "fsdp", [(i, i ^ 1) for i in range(lax.axis_size("fsdp"))])


def z_shift(a, k):
    n = lax.axis_size("dp")
    return lax.ppermute(a, "dp", [(i, (i + k) % n) for i in range(n)])


def z_gather(a):
    n = lax.axis_size("dp")
    me = lax.axis_index("dp")
    out = jnp.zeros((n, *a.shape), a.dtype)
    for k, part in enumerate([a] + [z_shift(a, k) for k in range(1, n)]):
        out = lax.dynamic_update_index_in_dim(out, part, lax.rem(me - k + n, n), 0)
    return out


def z_scatter(a):
    n = lax.axis_size("dp")
    me = lax.axis_index("dp")
    total = lax.dynamic_index_in_dim(a, me, 0, False).astype(F32)
    for k in range(1, n):
        total = total + z_shift(lax.dynamic_index_in_dim(a, lax.rem(me + k, n), 0, False), k).astype(F32)
    return total


def after(a, *earlier):
    return lax.optimization_barrier((a, *earlier))[0]


def plane_exchange(a):
    return lax.all_to_all(a, "fsdp", 0, 0, tiled=True, axis_index_groups=plane_groups(lax.axis_size("fsdp")))


def plane_gather(a):
    n = lax.axis_size("fsdp") // 2
    return plane_exchange(jnp.broadcast_to(a[None], (n, *a.shape)))


def core_order(core, own, other, axis):
    return jnp.where(core == 0, jnp.concatenate([own, other], axis), jnp.concatenate([other, own], axis))


def assemble(core, own, oth):
    own, oth = (jnp.transpose(a, (1, 0, 2, 3)).reshape(-1, a.shape[3]) for a in (own, oth))
    return core_order(core, own, oth, 1)


def half_of(a, which):
    wide = a.shape[1] // 2
    return lax.dynamic_slice_in_dim(a, which * wide, wide, 1)


class Gathered:
    def __init__(self, core, qkv, out, up, down, vectors):
        self.core = core
        self.rows = qkv.shape[0]
        self.widths = [w.shape[1] // 2 for w in (qkv, out, up)]
        self.size = vectors.shape[0]
        sides = jnp.stack(
            [
                jnp.concatenate([w[:, h * n : (h + 1) * n] for w, n in zip((qkv, out, up), self.widths)], 1)
                for h in range(2)
            ]
        )
        own = lax.dynamic_index_in_dim(sides, core, 0, False)
        chip = core_order(core, own, core_swap(lax.dynamic_index_in_dim(sides, 1 - core, 0, False)), 0)
        self.down = core_order(core, half_of(down, core), core_swap(half_of(down, 1 - core)), 0)
        vector_rows = jnp.zeros((8, self.widths[0]), BF).at[0, : self.size].set(vectors)
        self.first = jnp.concatenate([chip[:, : self.widths[0]], vector_rows], 0)
        self.second = chip[:, self.widths[0] :]

    def take_first(self, mine):
        other = core_swap(mine)
        rows = 2 * self.rows
        weight = assemble(self.core, mine[:, :, :rows], other[:, :, :rows])
        mine, other = (a[:, :, rows, : self.size] for a in (mine, other))
        every = jnp.where(self.core == 0, jnp.stack([mine, other], 2), jnp.stack([other, mine], 2))
        return weight, jnp.transpose(every, (1, 0, 2, 3)).reshape(-1, self.size)

    def take_second(self, mine):
        other = core_swap(mine)
        cut = self.widths[1]
        return (
            assemble(self.core, mine[..., :cut], other[..., :cut]),
            assemble(self.core, mine[..., cut:], other[..., cut:]),
        )

    def take_down(self, mine):
        mine = mine.reshape(-1, mine.shape[-1])
        return core_order(self.core, mine, core_swap(mine), 1)


def finish(core, total):
    rows = total.shape[0] // 2
    own = lax.dynamic_slice_in_dim(total, core * rows, rows, 0)
    other = core_swap(lax.dynamic_slice_in_dim(total, (1 - core) * rows, rows, 0))
    return core_order(core, own, other, 1)


def chip_parts(core, left, right):
    part = dot_tn(left, half_of(right, 1 - core)).astype(BF)

    def rest(left, right, sent):
        return (dot_tn(left, half_of(right, core)) + sent.astype(F32)).astype(BF)

    return part, rest


def summed(a):
    return jnp.sum(a.astype(F32), axis=0)


def by_plane(part):
    depth, plane = lax.axis_size("dp"), lax.axis_size("fsdp") // 2
    return jnp.transpose(part.reshape(depth, plane, -1, part.shape[1]), (1, 0, 2, 3))


def norm(residual):
    centre = residual - jnp.mean(residual, axis=-1, keepdims=True)
    scale = lax.rsqrt(jnp.mean(centre * centre, axis=-1, keepdims=True) + EPSILON)
    return centre * scale, scale


def norm_back(normed, scale, gained):
    inner = jnp.mean(gained * normed, axis=-1, keepdims=True)
    return scale * (gained - jnp.mean(gained, axis=-1, keepdims=True) - normed * inner)


def local(tokens, cotangent, key_mask, seq_lengths, block_pattern, deal_order, *shards):
    qkv_s, out_s, up_s, down_s = shards[:4]
    fsdp = lax.axis_size("fsdp")
    devices = fsdp * lax.axis_size("dp")
    me = lax.axis_index("fsdp")
    core = lax.rem(me, 2)
    count, piece, width = tokens.shape
    per = count // fsdp
    length = piece * fsdp
    fast = (2 * qkv_s.shape[0]) % 16 == 0

    def deal(a):
        return lax.all_to_all(a, "fsdp", split_axis=0, concat_axis=1, tiled=True)

    def give(a):
        return lax.all_to_all(a, "fsdp", split_axis=1, concat_axis=0, tiled=True)

    marks = key_mask.reshape(fsdp, per * piece)
    lengths = jnp.broadcast_to(seq_lengths[None], (fsdp, seq_lengths.shape[0]))
    notes = lax.all_to_all(jnp.concatenate([marks, lengths], 1), "fsdp", 0, 0, tiled=True)
    marks = notes[:, : per * piece].reshape(fsdp, per, piece).transpose(1, 0, 2).reshape(per, length)
    by_slot = notes[:, per * piece :].T.reshape(-1)
    own_ids = me * per + jnp.arange(per, dtype=jnp.int32)
    own_lengths = jnp.sum(jnp.where(deal_order[0][None, :] == own_ids[:, None], by_slot[None, :], 0), axis=1)
    positions = jnp.arange(length, dtype=jnp.int32)
    valid = ((marks == 1) & (positions[None, :] < own_lengths[:, None])).astype(F32)
    valid = valid.reshape(per, 2, 1, length // 2)

    vectors = jnp.concatenate(shards[4:])
    if fast:
        coming = Gathered(core, qkv_s, out_s, up_s, down_s, vectors)
        x3 = deal(tokens)
        first = z_gather(coming.first)
        second = z_gather(coming.second)
        first = plane_gather(after(first, x3))
        down = plane_gather(after(coming.down, first))
        down_w = coming.take_down(z_gather(down))
        second = plane_gather(after(second, down))
        g3 = deal(after(cotangent, second))
        qkv_w, every = coming.take_first(first)
        out_w, up_w = coming.take_second(second)
    else:
        x3 = deal(tokens)
        g3 = deal(cotangent)
        qkv_w, out_w, up_w, down_w, every = (
            lax.all_gather(w, BOTH, axis=0, tiled=True) for w in (qkv_s, out_s, up_s, down_s, vectors[None])
        )
    x = x3.reshape(per * length, width)
    sizes = [s.shape[0] for s in shards[4:]]
    starts = [sum(sizes[:i]) for i in range(len(sizes))]
    query_b, value_b, out_b, up_b, down_b, attn_gain, attn_shift, ffn_gain, ffn_shift = (
        every[:, a : a + n].astype(F32).reshape(1, -1) for a, n in zip(starts, sizes)
    )

    bias_all = jnp.concatenate([query_b, jnp.zeros_like(query_b), value_b], 1)
    project = (dot(x, qkv_w) + bias_all).astype(BF).reshape(per, length, 3 * width)
    mixed, probs = attention_fwd(project, valid, block_pattern)
    mixed = mixed.reshape(per * length, width)
    normed_one, scale_one = norm(x.astype(F32) + dot(mixed, out_w) + out_b)
    hidden = normed_one * attn_gain + attn_shift
    hidden_low = hidden.astype(BF)
    active, slope = ffn_up(hidden_low, up_w, up_b)
    normed_two, scale_two = norm(hidden + dot(active, down_w) + down_b)
    output = (normed_two * ffn_gain + ffn_shift).astype(BF).reshape(per, length, width)
    if fast:
        output = after(output, g3)
    output = give(output)

    g = g3.reshape(per * length, width).astype(F32)
    grad_ffn_gain = jnp.sum(g * normed_two, axis=0)
    grad_ffn_shift = jnp.sum(g, axis=0)
    grad_two = norm_back(normed_two, scale_two, g * ffn_gain)
    down_low = grad_two.astype(BF)
    grad_down_b = jnp.sum(down_low, axis=0, dtype=F32)

    if fast:
        part, rest = chip_parts(core, active, down_low)
        down_low = after(down_low, part)
        part = rest(active, down_low, core_swap(part))
        down_low = after(down_low, part)
        depth, plane = devices // fsdp, fsdp // 2
        down_part = z_scatter(part.reshape(depth, plane, -1, part.shape[1])).astype(BF)
    else:
        grad_down_w = dot_tn(active, down_low)
    up_low = (dot_nt(down_low, down_w) * slope.astype(F32)).astype(BF)
    grad_up_b = jnp.sum(up_low, axis=0, dtype=F32)
    if fast:
        part, rest = chip_parts(core, hidden_low, up_low)
        up_low = after(up_low, part)
        part = rest(hidden_low, up_low, core_swap(part))
        up_low = after(up_low, part)
        up_part = plane_exchange(after(by_plane(part), output))
        grad_up_w = finish(core, z_scatter(summed(up_part).astype(BF)))
    else:
        grad_up_w = dot_tn(hidden_low, up_low)
    grad_hidden = grad_two + dot_nt(up_low, up_w)
    grad_attn_gain = jnp.sum(grad_hidden * normed_one, axis=0)
    grad_attn_shift = jnp.sum(grad_hidden, axis=0)
    grad_one = norm_back(normed_one, scale_one, grad_hidden * attn_gain)
    out_low = grad_one.astype(BF)
    grad_out_b = jnp.sum(out_low, axis=0, dtype=F32)
    if fast:
        part, rest = chip_parts(core, mixed, out_low)
        out_low = after(out_low, part)
        part = rest(mixed, out_low, core_swap(part))
        out_low = after(out_low, part)
        out_part = plane_exchange(after(by_plane(part), up_part))
        grad_out_w = finish(core, z_scatter(summed(out_part).astype(BF)))
        down_part = plane_exchange(after(down_part, out_part))
        grad_down_w = finish(core, summed(down_part))
    else:
        grad_out_w = dot_tn(mixed, out_low)
    grad_mixed = dot_nt(out_low, out_w).astype(BF).reshape(per, length, width)
    grads = attention_bwd(project, probs, grad_mixed, block_pattern)
    grad_project = jnp.concatenate([d.reshape(per * length, width) for d in grads], 1)
    bias_sums = jnp.sum(grad_project, axis=0, dtype=F32)
    grad_vectors = (
        bias_sums[:width],
        bias_sums[2 * width :],
        grad_out_b,
        grad_up_b,
        grad_down_b,
        grad_attn_gain,
        grad_attn_shift,
        grad_ffn_gain,
        grad_ffn_shift,
    )
    laid = jnp.concatenate([v.reshape(devices, -1) for v in grad_vectors], 1)
    if fast:
        part, rest = chip_parts(core, x, grad_project)
        grad_project = after(grad_project, part)
        part = rest(x, grad_project, core_swap(part))
        grad_project = after(grad_project, part)
        laid = laid.reshape(depth * plane, 2, -1)
        sent = core_swap(lax.dynamic_index_in_dim(laid, 1 - core, 1, False).astype(BF))
        laid = lax.dynamic_index_in_dim(laid, core, 1, False) + sent.astype(F32)
        wide = part.shape[1]
        rows = jnp.zeros((depth * plane, 8, wide), BF).at[:, 0, : laid.shape[1]].set(laid.astype(BF))
        part = jnp.concatenate([part.reshape(depth * plane, -1, wide), rows], 1).reshape(-1, wide)
        qkv_part = plane_exchange(after(by_plane(part), down_part))
        total = z_scatter(summed(qkv_part).astype(BF))
        grad_qkv_w = finish(core, total[:-8])
        vector = total[-8, : laid.shape[1]]
    else:
        grad_qkv_w = dot_tn(x, grad_project)
        grad_qkv_w, grad_out_w, grad_up_w, grad_down_w, vector = (
            lax.psum_scatter(w.astype(BF), BOTH, scatter_dimension=0, tiled=True).astype(F32)
            for w in (grad_qkv_w, grad_out_w, grad_up_w, grad_down_w, laid)
        )
        vector = vector.reshape(-1)
    grad_tokens = (grad_one + dot_nt(grad_project, qkv_w)).astype(BF).reshape(per, length, width)
    if fast:
        grad_tokens = after(grad_tokens, qkv_part)
    grad_tokens = give(grad_tokens)
    vectors_out = [vector[a : a + n] for a, n in zip(starts, sizes)]
    return (output, grad_tokens, grad_qkv_w, grad_out_w, grad_up_w, grad_down_w, *vectors_out)


def solution(mesh):
    rows = P(BOTH, None)
    vec = P(BOTH)
    in_specs = (
        P("dp", "fsdp", None),
        P("dp", "fsdp", None),
        P("dp", "fsdp"),
        vec,
        P(),
        P("dp", None),
        *([rows] * 4),
        *([vec] * 9),
    )
    out_specs = (P("dp", "fsdp", None), P("dp", "fsdp", None), *([rows] * 4), *([vec] * 9))
    return jax.shard_map(local, mesh=mesh, in_specs=in_specs, out_specs=out_specs, check_vma=False)
```

time: 905 us -> 501 us (0.55)
  waiting for transfers between devices: 397 us -> 115 us
  matrix products: 178 us -> 91.4 us
  blocking collectives: 84.6 us -> 0 us
  starting transfers between devices: 43.1 us -> 103 us
  Pallas kernels: 0 us -> 56.8 us
  other arithmetic: 74.1 us -> 39 us
  between operations: 16.2 us -> 1.88 us
  local copies, waits for them, and re-layouts: 102 us -> 87.7 us
    reduce_scatter x4 -> x0, waiting for transfers between devices: 307 us -> none  [local(): lax.psum_scatter(totals, ('dp', 'fsdp'), scatter_dimension=0, tiled=True)]
    dot_general x36 -> x15, matrix products: 178 us -> 91.4 us  [the longest x8 37 us: dot_tn(): lax.dot_general(a, b, (((0,), (0,)), ((), ())), preferred_element_type=F32)]
    unnamed x2 -> x0, blocking collectives: 84.6 us -> none
    all_gather x4 -> x0, waiting for transfers between devices: 60 us -> none  [the longest x1 37.2 us: fetch_layer(): lax.all_gather(shards[2], ('dp', 'fsdp'), axis=0, tiled=True)]
    pallas_call x0 -> x3, Pallas kernels: none -> 56.8 us  [the longest x1 25 us: attention_bwd(): pl.pallas_call(functools.partial(attention_bwd_kernel, heads), grid_spec=...]
    ppermute x0 -> x35, starting transfers between devices: none -> 55.2 us  [the longest x21 51.9 us: z_shift(): return lax.ppermute(a, 'dp', [(i, (i + k) % n) for i in range(n)])]
    unnamed x219 -> x61, local copies, waits for them, and re-layouts: 50.2 us -> 2.81 us
    all_to_all x10 -> x12, waiting for transfers between devices: 27.7 us -> 71.5 us  [the longest x7 34.4 us: plane_exchange(): lax.all_to_all(a, 'fsdp', 0, 0, tiled=True, axis_index_groups=plane_group...]
  transfers between devices with their start and end apart: 18 -> 47, of which waited for: 9 -> 17; matrix products, arithmetic and copies ran while one was open for 29% -> 33% of each run, Pallas kernels for 0% -> 11%
where the time goes in v1:
time: 501 us; the launch traced here: 495 us
  waiting for transfers between devices  115 us (23%)
  starting transfers between devices  103 us (21%)
  matrix products  91.4 us (18%)
  local copies, waits for them, and re-layouts  87.7 us (18%)
  Pallas kernels  56.8 us (11%)
  other arithmetic  39 us (8%)
    ppermute x21, starting transfers between devices, z_shift(): return lax.ppermute(a, 'dp', [(i, (i + k) % n) for i in range(n)])  51.9 us
    ppermute x21, waiting for transfers between devices, z_shift(): return lax.ppermute(a, 'dp', [(i, (i + k) % n) for i in range(n)])  38.7 us
    dot_general x8, matrix products, dot_tn(): lax.dot_general(a, b, (((0,), (0,)), ((), ())), preferred_element_type=F32)  37 us
    all_to_all x7, waiting for transfers between devices, plane_exchange(): lax.all_to_all(a, 'fsdp', 0, 0, tiled=True, axis_index_groups=plane_group...  34.4 us
    dot_general x4, matrix products, dot_nt(): lax.dot_general(a, b, (((1,), (1,)), ((), ())), preferred_element_type=F32)  32.2 us
    all_to_all x7, starting transfers between devices, plane_exchange(): lax.all_to_all(a, 'fsdp', 0, 0, tiled=True, axis_index_groups=plane_group...  27.1 us
    pallas_call x1, Pallas kernels, attention_bwd(): pl.pallas_call(functools.partial(attention_bwd_kernel, heads), grid_spec=...  25 us
    dot_general x3, matrix products, dot(): return jnp.dot(a, b, preferred_element_type=F32)  22.1 us
  transfers between devices with their start and end apart: 47, of which 17 were waited for; matrix products, arithmetic and copies ran while one was open for 33% of the time, Pallas kernels for 11%

profile of v1, /device:TPU:0, one launch (start us, length us, event | category | flops | bytes accessed | tf_op | source)
XLA Modules:
  0.0 494.6 jit_solution(15561430102171467595)
XLA Ops:
  3.9 6.1 %concatenate.119 = bf16[288]{0:T(512)(128)(2,1)S(1)} concatenate(bf16[24]{0:T(256)(128)(2,1)} %param.33, bf16[24]{0:T(256)(128)(2,1)} %param.34, bf16[24]{0:T(256)(128)(2,1)} %param.35, bf16[96]{0:T(256)(128)(2,1)} %param.36, bf16[24]{0:T(256)(128)(2,1)} %param.37, bf16[24]{0:T(256)(128)(2,1)} %param.38, bf16[24]{0:T(256)(128)(2,1)} %param.39, bf16[24]{0:T(256)(128)(2,1)} %param.40, ...), dimensions={0} | concatenate | bytes 1152 | tf_op jit(solution)/shard_map/concatenate | solution.py:340
  17.7 4.6 collective-permute-done.1
  31.2 23.2 %all-to-all-done.1 = bf16[4,4,56,1152]{3,2,1,0:T(8,128)(2,1)S(1)} async-done(((bf16[4,4,56,1152]{3,2,1,0:T(8,128)(2,1)}), bf16[4,4,56,1152]{3,2,1,0:T(8,128)(2,1)S(1)}, u32[]{:S(2)}, u32[]{:S(2)}) %all-to-all-start.1) | async-done | bytes 2064416 | tf_op jit(solution)/shard_map/all_to_all | solution.py:214
  57.7 4.6 all-to-all-done.2
  67.3 4.7 collective-permute-start.6
  72.1 3.8 collective-permute-start.7
  75.9 4.3 all-to-all-start
  87.1 14.2 %all-to-all-done = bf16[16,64,768]{2,1,0:T(8,128)(2,1)} async-done(((bf16[16,64,768]{2,1,0:T(8,128)(2,1)}), bf16[16,64,768]{2,1,0:T(8,128)(2,1)}, u32[]{:S(2)}, u32[]{:S(2)}) %all-to-all-start) | async-done | bytes 1572896 | tf_op jit(solution)/shard_map/all_to_all | solution.py:324
  137.6 22.8 %collective-permute-done.11 = bf16[4,192,384]{2,1,0:T(8,128)(2,1)S(1)} collective-permute-done((bf16[4,192,384]{2,1,0:T(8,128)(2,1)S(1)}, bf16[4,192,384]{2,1,0:T(8,128)(2,1)S(1)}, u32[]{:S(2)}, u32[]{:S(2)}) %collective-permute-start.11) | collective-permute-done | bytes 589856 | tf_op jit(solution)/shard_map/ppermute | solution.py:188
  169.8 4.5 all-to-all-start.6
  174.3 9.6 %add_convert_fusion = bf16[2304,1024]{0,1:T(8,128)(2,1)} fusion(bf16[1024,768]{1,0:T(8,128)(2,1)} %bitcast.222, f32[2304]{0:T(1024)S(1)} %fusion.49, bf16[768,1152]{1,0:T(8,128)(2,1)} %bitcast.217, bf16[768,1152]{1,0:T(8,128)(2,1)} %bitcast.215, pred[]{:T(512)S(6)} %eq.50), kind=kOutput, calls=%fused_computation.3 | convolution fusion | flops 3644522496 | bytes 9839617 | tf_op jit(solution)/shard_map/dot_general | solution.py:21
  185.2 17.0 %attention_fwd.1 = (bf16[2,512,768]{2,1,0:T(8,128)(2,1)}, bf16[2,12,2,256,256]{4,3,2,1,0:T(8,128)(2,1)}) custom-call(s32[12]{0:T(128)} %pattern.3, bf16[2,512,2304]{2,1,0:T(8,128)(2,1)} %bitcast.197, bf16[2,512,2304]{2,1,0:T(8,128)(2,1)} %bitcast.198, bf16[2,512,2304]{2,1,0:T(8,128)(2,1)} %bitcast.199, f32[2,2,1,256]{3,2,1,0:T(1,128)} %and_convert_fusion.valid_ref), custom_call_target="tpu_custom_call" | custom-call | flops 3221225472 | bytes 12000000 | tf_op jit(solution)/shard_map/attention_fwd/pallas_call | solution.py:63
  219.0 14.9 %ffn_up.1 = (bf16[1024,3072]{1,0:T(8,128)(2,1)}, bf16[1024,3072]{1,0:T(8,128)(2,1)}) custom-call(bf16[1024,768]{1,0:T(8,128)(2,1)} %fusion.7.h_ref, bf16[768,3072]{1,0:T(8,128)(2,1)} %maximum_select_fusion.w_ref, f32[1,3072]{1,0:T(1,128)} %reshape.405.b_ref), custom_call_target="tpu_custom_call" | custom-call | flops 4957667328 | bytes 20000000 | tf_op jit(solution)/shard_map/ffn_up/pallas_call | solution.py:160
  233.9 10.9 %fusion.62 = (f32[1024]{0:T(1024)S(1)}, f32[1024,768]{1,0:T(8,128)S(1)}) fusion(f32[768]{0:T(1024)S(1)} %reshape.406, bf16[1024,3072]{1,0:T(8,128)(2,1)} %get-tuple-element.65, bf16[3072,384]{1,0:T(8,128)(2,1)} %collective-permute-done.13, bf16[3072,384]{1,0:T(8,128)(2,1)} %bitcast.44, pred[]{:T(512)S(6)} %eq.50, f32[768]{0:T(1024)S(1)} %reshape.403, ...), kind=kOutput, calls=%fused_computation.191 | convolution fusion | flops 4858575872 | bytes 17323008 | tf_op jit(solution)/shard_map/dot_general | solution.py:21
  250.8 5.2 %convolution_convert_fusion = bf16[3072,384]{1,0:T(8,128)(2,1)} fusion(bf16[1024,3072]{1,0:T(8,128)(2,1)S(1)} %bitcast.245, bf16[1024,768]{1,0:T(8,128)(2,1)S(1)} %get-tuple-element.68, s32[]{:T(128)S(6)} %select_n.201), kind=kOutput, calls=%fused_computation.9 | convolution fusion | flops 2417098752 | bytes 9437188 | tf_op jit(solution)/shard_map/dot_general | solution.py:29
  256.5 4.5 collective-permute-done.14
  261.0 8.6 %add_convert_fusion.2 = bf16[3072,384]{1,0:T(8,128)(2,1)} fusion(bf16[3072,384]{1,0:T(8,128)(2,1)} %collective-permute-done.14, bf16[1024,3072]{1,0:T(8,128)(2,1)} %get-tuple-element.65, bf16[1024,768]{1,0:T(8,128)(2,1)} %copy-done.9, s32[]{:T(128)S(6)} %select_n.200), kind=kOutput, calls=%fused_computation.8 | convolution fusion | flops 2419458048 | bytes 11796484 | tf_op jit(solution)/shard_map/dot_general | solution.py:29
  269.6 10.1 %convert_reduce_fusion = (f32[3072]{0:T(1024)}, bf16[1024,3072]{1,0:T(8,128)(2,1)S(1)}) fusion(bf16[1024,3072]{1,0:T(8,128)(2,1)} %get-tuple-element.69, bf16[1024,768]{1,0:T(8,128)(2,1)S(1)} %copy-done.10, bf16[3072,384]{1,0:T(8,128)(2,1)} %collective-permute-done.13, bf16[3072,384]{1,0:T(8,128)(2,1)} %bitcast.44, pred[]{:T(512)S(6)} %eq.50), kind=kOutput, calls=%fused_computation | convolution fusion | flops 4868797440 | bytes 18886656 | tf_op jit(solution)/shard_map/dot_general | solution.py:25
  279.7 4.0 convolution_convert_fusion.1
  284.1 4.2 copy.111
  288.3 4.5 all-to-all-start.5
  292.7 7.3 %add_convert_fusion.1 = bf16[768,1536]{1,0:T(8,128)(2,1)} fusion(bf16[768,1536]{1,0:T(8,128)(2,1)} %collective-permute-done.15, bf16[1024,768]{1,0:T(8,128)(2,1)} %fusion.7.h_ref, bf16[1024,3072]{1,0:T(8,128)(2,1)} %copy-done.26, s32[]{:T(128)S(6)} %select_n.209), kind=kOutput, calls=%fused_computation.7 | convolution fusion | flops 2419458048 | bytes 9437188 | tf_op jit(solution)/shard_map/dot_general | solution.py:29
  300.0 10.2 %multiply_reduce_fusion = (f32[768]{0:T(1024)}, f32[1024]{0:T(1024)S(1)}, f32[1024]{0:T(1024)S(1)}, f32[768]{0:T(1024)}, f32[1024,768]{1,0:T(8,128)S(1)}) fusion(f32[1024,768]{1,0:T(8,128)S(1)} %get-tuple-element.149, f32[1024]{0:T(1024)S(1)} %add_rsqrt_fusion.1, f32[1024]{0:T(1024)S(1)} %broadcast_multiply_fusion.4, f32[768]{0:T(1024)S(1)} %reshape.402, ...), kind=kOutput, calls=%fused_computation.18 | convolution fusion | flops 4839698432 | bytes 20472832 | tf_op jit(solution)/shard_map/dot_general | solution.py:25
  320.1 13.2 %collective-permute-start.19 = (bf16[4,192,384]{2,1,0:T(8,128)(2,1)}, bf16[4,192,384]{2,1,0:T(8,128)(2,1)S(1)}, u32[]{:S(2)}, u32[]{:S(2)}) collective-permute-start(bf16[4,192,384]{2,1,0:T(8,128)(2,1)} %get-tuple-element.100), channel_id=1, source_target_pairs={{0,8},{8,16},{16,24},{24,0},{1,9},{9,17},{17,25},{25,1},{2,10},{10... | collective-permute-start | bytes 1769480 | tf_op jit(solution)/shard_map/ppermute | solution.py:188
  338.4 4.1 all-to-all-start.7
  348.1 25.0 %attention_bwd.1 = (bf16[2,512,768]{2,1,0:T(8,128)(2,1)}, bf16[2,512,768]{2,1,0:T(8,128)(2,1)}, bf16[2,512,768]{2,1,0:T(8,128)(2,1)}) custom-call(s32[12]{0:T(128)} %pattern.3, bf16[2,512,2304]{2,1,0:T(8,128)(2,1)} %bitcast.200, bf16[2,512,2304]{2,1,0:T(8,128)(2,1)} %bitcast.201, bf16[2,512,2304]{2,1,0:T(8,128)(2,1)} %bitcast.202, ...), custom_call_target="tpu_custom_call" | custom-call | flops 6442450944 | bytes 16000000 | tf_op jit(solution)/shard_map/attention_bwd/pallas_call | solution.py:122
  395.8 4.2 all-to-all-start.8
  413.1 4.7 add_convert_fusion.3
  423.1 4.2 all-to-all-start.10
  441.9 9.1 %all-to-all-done.10 = bf16[4,4,56,1152]{3,2,1,0:T(8,128)(2,1)S(1)} async-done(((bf16[4,4,56,1152]{3,2,1,0:T(8,128)(2,1)}), bf16[4,4,56,1152]{3,2,1,0:T(8,128)(2,1)S(1)}, u32[]{:S(2)}, u32[]{:S(2)}) %all-to-all-start.10) | async-done | bytes 2064416 | tf_op jit(solution)/shard_map/all_to_all | solution.py:214
  455.6 9.3 %add_convert_fusion.4 = bf16[1024,768]{1,0:T(8,128)(2,1)S(1)} fusion(f32[1024,768]{1,0:T(8,128)} %get-tuple-element.96, bf16[1024,2304]{1,0:T(8,128)(2,1)} %copy-done.2, bf16[768,1152]{1,0:T(8,128)(2,1)} %bitcast.218, bf16[768,1152]{1,0:T(8,128)(2,1)} %bitcast.216, pred[]{:T(512)S(6)} %eq.50), kind=kOutput, calls=%fused_computation.21 | convolution fusion | flops 3641376768 | bytes 12976129 | tf_op jit(solution)/shard_map/dot_general | solution.py:25
  474.5 18.4 %all-to-all-done.11 = bf16[2,512,768]{2,0,1:T(2,128)(2,1)S(1)} async-done(((bf16[2,512,768]{2,0,1:T(2,128)(2,1)}), bf16[2,512,768]{2,0,1:T(2,128)(2,1)S(1)}, u32[]{:S(2)}, u32[]{:S(2)}) %all-to-all-start.11) | async-done | bytes 1572896 | tf_op jit(solution)/shard_map/all_to_all | solution.py:327
  (285 shorter events, 196.8 us)
Async XLA Ops:
  10.1 13.6 %collective-permute-start.2 = (bf16[56,1152]{1,0:T(8,128)(2,1)S(1)}, bf16[56,1152]{1,0:T(8,128)(2,1)S(1)}, u32[]{:S(2)}, u32[]{:S(2)}) collective-permute-start(bf16[56,1152]{1,0:T(8,128)(2,1)S(1)} %fusion.34), channel_id=1, source_target_pairs={{0,16},{8,24},{16,0},{24,8},{1,17},{9,25},{17,1},{25,9},{2,18},{10... | collective-permute-start | bytes 387080 | tf_op jit(solution)/shard_map/ppermute | solution.py:188
  26.6 27.7 %all-to-all-start.1 = ((bf16[4,4,56,1152]{3,2,1,0:T(8,128)(2,1)}), bf16[4,4,56,1152]{3,2,1,0:T(8,128)(2,1)S(1)}, u32[]{:S(2)}, u32[]{:S(2)}) async-start(bf16[4,4,56,1152]{3,2,1,0:T(8,128)(2,1)} %broadcast_in_dim.107), calls=%async_computation.1 | async-start | bytes 4128768 | tf_op jit(solution)/shard_map/all_to_all | solution.py:214
  30.4 27.3 %collective-permute-start.8 = (bf16[96,384]{1,0:T(8,128)(2,1)S(1)}, bf16[96,384]{1,0:T(8,128)(2,1)S(1)}, u32[]{:S(2)}, u32[]{:S(2)}) collective-permute-start(bf16[96,384]{1,0:T(8,128)(2,1)S(1)} %get-tuple-element.129), channel_id=1, source_target_pairs={{0,1},{1,0},{2,3},{3,2},{4,5},{5,4},{6,7},{7,6},{8,9},{9,8},{10,11... | collective-permute-start | bytes 221192 | tf_op jit(solution)/shard_map/ppermute | solution.py:183
  63.2 12.8 %all-to-all-start.3 = ((bf16[4,192,384]{2,1,0:T(8,128)(2,1)}), bf16[4,192,384]{2,1,0:T(8,128)(2,1)S(1)}, u32[]{:S(2)}, u32[]{:S(2)}) async-start(bf16[4,192,384]{2,1,0:T(8,128)(2,1)} %broadcast_in_dim.118), calls=%async_computation.3 | async-start | bytes 1179648 | tf_op jit(solution)/shard_map/all_to_all | solution.py:214
  67.3 17.9 %collective-permute-start.6 = (bf16[48,1920]{1,0:T(8,128)(2,1)}, bf16[48,1920]{1,0:T(8,128)(2,1)}, u32[]{:S(2)}, u32[]{:S(2)}) collective-permute-start(bf16[48,1920]{1,0:T(8,128)(2,1)} %slice.266), channel_id=1, source_target_pairs={{0,16},{8,24},{16,0},{24,8},{1,17},{9,25},{17,1},{25,9},{2,18},{10... | collective-permute-start | bytes 552968 | tf_op jit(solution)/shard_map/ppermute | solution.py:188
  72.1 14.1 %collective-permute-start.7 = (bf16[48,1920]{1,0:T(8,128)(2,1)}, bf16[48,1920]{1,0:T(8,128)(2,1)}, u32[]{:S(2)}, u32[]{:S(2)}) collective-permute-start(bf16[48,1920]{1,0:T(8,128)(2,1)} %slice.266), channel_id=1, source_target_pairs={{0,24},{8,0},{16,8},{24,16},{1,25},{9,1},{17,9},{25,17},{2,26},{10... | collective-permute-start | bytes 552968 | tf_op jit(solution)/shard_map/ppermute | solution.py:188
  75.9 25.4 %all-to-all-start = ((bf16[16,64,768]{2,1,0:T(8,128)(2,1)}), bf16[16,64,768]{2,1,0:T(8,128)(2,1)}, u32[]{:S(2)}, u32[]{:S(2)}) async-start(bf16[16,64,768]{2,1,0:T(8,128)(2,1)} %param.23), calls=%async_computation | async-start | bytes 3145728 | tf_op jit(solution)/shard_map/all_to_all | solution.py:324
  103.1 58.2 %all-to-all-start.4 = ((bf16[4,4,48,1920]{3,2,1,0:T(8,128)(2,1)}), bf16[4,4,48,1920]{3,2,1,0:T(8,128)(2,1)S(1)}, u32[]{:S(2)}, u32[]{:S(2)}) async-start(bf16[4,4,48,1920]{3,2,1,0:T(8,128)(2,1)} %broadcast_in_dim.119), calls=%async_computation.4 | async-start | bytes 5898240 | tf_op jit(solution)/shard_map/all_to_all | solution.py:214
  109.8 55.8 %collective-permute-start.4 = (bf16[4,4,56,1152]{3,2,0,1:T(8,128)(2,1)}, bf16[4,4,56,1152]{3,2,0,1:T(8,128)(2,1)}, u32[]{:S(2)}, u32[]{:S(2)}) collective-permute-start(bf16[4,4,56,1152]{3,2,0,1:T(8,128)(2,1)} %copy.102), channel_id=1, source_target_pairs={{0,1},{1,0},{2,3},{3,2},{4,5},{5,4},{6,7},{7,6},{8,9},{9,8},{10,11... | collective-permute-start | bytes 6193160 | tf_op jit(solution)/shard_map/ppermute | solution.py:183
  117.5 19.2 %collective-permute-start.10 = (bf16[4,192,384]{2,1,0:T(8,128)(2,1)S(1)}, bf16[4,192,384]{2,1,0:T(8,128)(2,1)S(1)}, u32[]{:S(2)}, u32[]{:S(2)}) collective-permute-start(bf16[4,192,384]{2,1,0:T(8,128)(2,1)S(1)} %all-to-all-done.3), channel_id=1, source_target_pairs={{0,8},{8,16},{16,24},{24,0},{1,9},{9,17},{17,25},{25,1},{2,10},{10... | collective-permute-start | bytes 1769480 | tf_op jit(solution)/shard_map/ppermute | solution.py:188
  120.8 39.5 %collective-permute-start.11 = (bf16[4,192,384]{2,1,0:T(8,128)(2,1)S(1)}, bf16[4,192,384]{2,1,0:T(8,128)(2,1)S(1)}, u32[]{:S(2)}, u32[]{:S(2)}) collective-permute-start(bf16[4,192,384]{2,1,0:T(8,128)(2,1)S(1)} %all-to-all-done.3), channel_id=1, source_target_pairs={{0,16},{8,24},{16,0},{24,8},{1,17},{9,25},{17,1},{25,9},{2,18},{10... | collective-permute-start | bytes 1769480 | tf_op jit(solution)/shard_map/ppermute | solution.py:188
  131.2 31.9 %collective-permute-start.12 = (bf16[4,192,384]{2,1,0:T(8,128)(2,1)S(1)}, bf16[4,192,384]{2,1,0:T(8,128)(2,1)}, u32[]{:S(2)}, u32[]{:S(2)}) collective-permute-start(bf16[4,192,384]{2,1,0:T(8,128)(2,1)S(1)} %all-to-all-done.3), channel_id=1, source_target_pairs={{0,24},{8,0},{16,8},{24,16},{1,25},{9,1},{17,9},{25,17},{2,26},{10... | collective-permute-start | bytes 1769480 | tf_op jit(solution)/shard_map/ppermute | solution.py:188
  163.1 45.3 %collective-permute-start.9 = (bf16[4,4,48,1920]{3,2,0,1:T(8,128)(2,1)}, bf16[4,4,48,1920]{3,2,0,1:T(8,128)(2,1)}, u32[]{:S(2)}, u32[]{:S(2)}) collective-permute-start(bf16[4,4,48,1920]{3,2,0,1:T(8,128)(2,1)} %copy.108), channel_id=1, source_target_pairs={{0,1},{1,0},{2,3},{3,2},{4,5},{5,4},{6,7},{7,6},{8,9},{9,8},{10,11... | collective-permute-start | bytes 8847368 | tf_op jit(solution)/shard_map/ppermute | solution.py:183
  165.1 68.8 %collective-permute-start.13 = (bf16[3072,384]{1,0:T(8,128)(2,1)}, bf16[3072,384]{1,0:T(8,128)(2,1)}, u32[]{:S(2)}, u32[]{:S(2)}) collective-permute-start(bf16[3072,384]{1,0:T(8,128)(2,1)} %bitcast.44), channel_id=1, source_target_pairs={{0,1},{1,0},{2,3},{3,2},{4,5},{5,4},{6,7},{7,6},{8,9},{9,8},{10,11... | collective-permute-start | bytes 7077896 | tf_op jit(solution)/shard_map/ppermute | solution.py:183
  169.8 36.1 %all-to-all-start.6 = ((bf16[16,64,768]{2,1,0:T(8,128)(2,1)}), bf16[16,64,768]{2,1,0:T(8,128)(2,1)}, u32[]{:S(2)}, u32[]{:S(2)}) async-start(bf16[16,64,768]{2,1,0:T(8,128)(2,1)} %param.24), calls=%async_computation.6 | async-start | bytes 3145728 | tf_op jit(solution)/shard_map/all_to_all | solution.py:324
  288.3 27.6 %all-to-all-start.5 = ((bf16[2,512,768]{2,0,1:T(2,128)(2,1)}), bf16[2,512,768]{2,0,1:T(2,128)(2,1)}, u32[]{:S(2)}, u32[]{:S(2)}) async-start(bf16[2,512,768]{2,0,1:T(2,128)(2,1)} %copy.111), calls=%async_computation.5 | async-start | bytes 3145728 | tf_op jit(solution)/shard_map/all_to_all | solution.py:327
  315.4 27.2 %collective-permute-start.16 = (bf16[768,384]{1,0:T(8,128)(2,1)S(1)}, bf16[768,384]{1,0:T(8,128)(2,1)}, u32[]{:S(2)}, u32[]{:S(2)}) collective-permute-start(bf16[768,384]{1,0:T(8,128)(2,1)S(1)} %convolution_convert_fusion.4), channel_id=1, source_target_pairs={{0,1},{1,0},{2,3},{3,2},{4,5},{5,4},{6,7},{7,6},{8,9},{9,8},{10,11... | collective-permute-start | bytes 1769480 | tf_op jit(solution)/shard_map/ppermute | solution.py:183
  320.1 67.0 %collective-permute-start.19 = (bf16[4,192,384]{2,1,0:T(8,128)(2,1)}, bf16[4,192,384]{2,1,0:T(8,128)(2,1)S(1)}, u32[]{:S(2)}, u32[]{:S(2)}) collective-permute-start(bf16[4,192,384]{2,1,0:T(8,128)(2,1)} %get-tuple-element.100), channel_id=1, source_target_pairs={{0,8},{8,16},{16,24},{24,0},{1,9},{9,17},{17,25},{25,1},{2,10},{10... | collective-permute-start | bytes 1769480 | tf_op jit(solution)/shard_map/ppermute | solution.py:188
  333.3 53.8 %collective-permute-start.21 = (bf16[4,192,384]{2,1,0:T(8,128)(2,1)}, bf16[4,192,384]{2,1,0:T(8,128)(2,1)}, u32[]{:S(2)}, u32[]{:S(2)}) collective-permute-start(bf16[4,192,384]{2,1,0:T(8,128)(2,1)} %get-tuple-element.101), channel_id=1, source_target_pairs={{0,24},{8,0},{16,8},{24,16},{1,25},{9,1},{17,9},{25,17},{2,26},{10... | collective-permute-start | bytes 1769480 | tf_op jit(solution)/shard_map/ppermute | solution.py:188
  336.2 51.8 %collective-permute-start.20 = (bf16[4,192,384]{2,1,0:T(8,128)(2,1)}, bf16[4,192,384]{2,1,0:T(8,128)(2,1)}, u32[]{:S(2)}, u32[]{:S(2)}) collective-permute-start(bf16[4,192,384]{2,1,0:T(8,128)(2,1)} %get-tuple-element.102), channel_id=1, source_target_pairs={{0,16},{8,24},{16,0},{24,8},{1,17},{9,25},{17,1},{25,9},{2,18},{10... | collective-permute-start | bytes 1769480 | tf_op jit(solution)/shard_map/ppermute | solution.py:188
  338.4 57.4 %all-to-all-start.7 = ((bf16[4,4,48,1536]{3,2,1,0:T(8,128)(2,1)}), bf16[4,4,48,1536]{3,2,1,0:T(8,128)(2,1)S(1)}, u32[]{:S(2)}, u32[]{:S(2)}) async-start(bf16[4,4,48,1536]{3,2,1,0:T(8,128)(2,1)} %bitcast.205), calls=%async_computation.7 | async-start | bytes 4718592 | tf_op jit(solution)/shard_map/all_to_all | solution.py:214
  379.9 33.2 %collective-permute-start.17 = (bf16[768,1152]{0,1:T(8,128)(2,1)}, bf16[768,1152]{0,1:T(8,128)(2,1)}, u32[]{:S(2)}, u32[]{:S(2)}) collective-permute-start(bf16[768,1152]{0,1:T(8,128)(2,1)} %fusion.6), channel_id=1, source_target_pairs={{0,1},{1,0},{2,3},{3,2},{4,5},{5,4},{6,7},{7,6},{8,9},{9,8},{10,11... | collective-permute-start | bytes 5308424 | tf_op jit(solution)/shard_map/ppermute | solution.py:183
  395.8 13.5 %all-to-all-start.8 = ((bf16[4,4,48,384]{3,2,1,0:T(8,128)(2,1)}), bf16[4,4,48,384]{3,2,1,0:T(8,128)(2,1)S(1)}, u32[]{:S(2)}, u32[]{:S(2)}) async-start(bf16[4,4,48,384]{3,2,1,0:T(8,128)(2,1)} %bitcast.212), calls=%async_computation.8 | async-start | bytes 1179648 | tf_op jit(solution)/shard_map/all_to_all | solution.py:214
  403.2 24.1 %collective-permute-start.30 = (bf16[48,1536]{1,0:T(8,128)(2,1)}, bf16[48,1536]{1,0:T(8,128)(2,1)}, u32[]{:S(2)}, u32[]{:S(2)}) collective-permute-start(bf16[48,1536]{1,0:T(8,128)(2,1)} %get-tuple-element.103), channel_id=1, source_target_pairs={{0,8},{8,16},{16,24},{24,0},{1,9},{9,17},{17,25},{25,1},{2,10},{10... | collective-permute-start | bytes 442376 | tf_op jit(solution)/shard_map/ppermute | solution.py:188
  404.9 22.4 %collective-permute-start.32 = (bf16[48,1536]{1,0:T(8,128)(2,1)}, bf16[48,1536]{1,0:T(8,128)(2,1)}, u32[]{:S(2)}, u32[]{:S(2)}) collective-permute-start(bf16[48,1536]{1,0:T(8,128)(2,1)} %get-tuple-element.104), channel_id=1, source_target_pairs={{0,24},{8,0},{16,8},{24,16},{1,25},{9,1},{17,9},{25,17},{2,26},{10... | collective-permute-start | bytes 442376 | tf_op jit(solution)/shard_map/ppermute | solution.py:188
  407.1 20.3 %collective-permute-start.31 = (bf16[48,1536]{1,0:T(8,128)(2,1)}, bf16[48,1536]{1,0:T(8,128)(2,1)}, u32[]{:S(2)}, u32[]{:S(2)}) collective-permute-start(bf16[48,1536]{1,0:T(8,128)(2,1)} %get-tuple-element.105), channel_id=1, source_target_pairs={{0,16},{8,24},{16,0},{24,8},{1,17},{9,25},{17,1},{25,9},{2,18},{10... | collective-permute-start | bytes 442376 | tf_op jit(solution)/shard_map/ppermute | solution.py:188
  423.1 27.9 %all-to-all-start.10 = ((bf16[4,4,56,1152]{3,2,1,0:T(8,128)(2,1)}), bf16[4,4,56,1152]{3,2,1,0:T(8,128)(2,1)S(1)}, u32[]{:S(2)}, u32[]{:S(2)}) async-start(bf16[4,4,56,1152]{3,2,1,0:T(8,128)(2,1)} %copy.120), calls=%async_computation.10 | async-start | bytes 4128768 | tf_op jit(solution)/shard_map/all_to_all | solution.py:214
  441.7 23.2 %collective-permute-start.34 = (f32[96,384]{1,0:T(8,128)S(1)}, f32[96,384]{1,0:T(8,128)S(1)}, u32[]{:S(2)}, u32[]{:S(2)}) collective-permute-start(f32[96,384]{1,0:T(8,128)S(1)} %get-tuple-element.110), channel_id=1, source_target_pairs={{0,1},{1,0},{2,3},{3,2},{4,5},{5,4},{6,7},{7,6},{8,9},{9,8},{10,11... | collective-permute-start | bytes 442376 | tf_op jit(solution)/shard_map/ppermute | solution.py:183
  451.7 20.3 %collective-permute-start.22 = (bf16[56,1152]{1,0:T(8,128)(2,1)S(1)}, bf16[56,1152]{1,0:T(8,128)(2,1)S(1)}, u32[]{:S(2)}, u32[]{:S(2)}) collective-permute-start(bf16[56,1152]{1,0:T(8,128)(2,1)S(1)} %get-tuple-element.106), channel_id=1, source_target_pairs={{0,8},{8,16},{16,24},{24,0},{1,9},{9,17},{17,25},{25,1},{2,10},{10... | collective-permute-start | bytes 387080 | tf_op jit(solution)/shard_map/ppermute | solution.py:188
  452.7 19.3 %collective-permute-start.24 = (bf16[56,1152]{1,0:T(8,128)(2,1)S(1)}, bf16[56,1152]{1,0:T(8,128)(2,1)S(1)}, u32[]{:S(2)}, u32[]{:S(2)}) collective-permute-start(bf16[56,1152]{1,0:T(8,128)(2,1)S(1)} %get-tuple-element.107), channel_id=1, source_target_pairs={{0,24},{8,0},{16,8},{24,16},{1,25},{9,1},{17,9},{25,17},{2,26},{10... | collective-permute-start | bytes 387080 | tf_op jit(solution)/shard_map/ppermute | solution.py:188
  455.6 16.4 %collective-permute-start.23 = (bf16[56,1152]{1,0:T(8,128)(2,1)S(1)}, bf16[56,1152]{1,0:T(8,128)(2,1)S(1)}, u32[]{:S(2)}, u32[]{:S(2)}) collective-permute-start(bf16[56,1152]{1,0:T(8,128)(2,1)S(1)} %get-tuple-element.108), channel_id=1, source_target_pairs={{0,16},{8,24},{16,0},{24,8},{1,17},{9,25},{17,1},{25,9},{2,18},{10... | collective-permute-start | bytes 387080 | tf_op jit(solution)/shard_map/ppermute | solution.py:188
  468.4 24.5 %all-to-all-start.11 = ((bf16[2,512,768]{2,0,1:T(2,128)(2,1)}), bf16[2,512,768]{2,0,1:T(2,128)(2,1)S(1)}, u32[]{:S(2)}, u32[]{:S(2)}) async-start(bf16[2,512,768]{2,0,1:T(2,128)(2,1)} %copy.121), calls=%async_computation.11 | async-start | bytes 3145728 | tf_op jit(solution)/shard_map/all_to_all | solution.py:327
  (44 other events, 327.4 us)
